TPU v7x, 32 devices: a whole 2x2x4 slice. The times are simulated.
32 devices in a mesh: section: 2 (over x), expert: 16 (over z, y, core).
Axes of the slice: x: 2, y: 2, z: 4, core: 2. Of those that a mesh axis runs over, the one named last changes fastest.
Arguments:
- tokens: bfloat16 [2, 2, 1024, 7168], P('section', None, 'expert'), may hold values from -6 to 6
- expert_ids: int32 [2, 2, 1024, 2], P('section', None, 'expert'), may hold values from 0 to 3, all different within a row; in each aligned block of 64 rows (0 to 63, 64 to 127, ..., all dimensions but the last counted through in order) at most 40 rows name the same one
- gate_weights: float32 [2, 2, 1024, 2], P('section', None, 'expert'), may hold values from 0.1 to 1
- w_gate: bfloat16 [2, 16, 7168, 512], P('section', 'expert'), may hold values from -0.0625 to 0.0625
- w_up: bfloat16 [2, 16, 7168, 512], P('section', 'expert'), may hold values from -0.0625 to 0.0625
- w_down: bfloat16 [2, 16, 512, 7168], P('section', 'expert'), may hold values from -0.125 to 0.125
Outputs:
- passed: bfloat16 [2, 2, 1024, 7168], P('section', None, 'expert')
Inputs may be any that keep to these rules, and one draw needn't show every extreme that they name: `expert_ids`: in each aligned block of 64 tokens of one micro-batch (the tokens of one device), the 2 experts of a token differ, and no expert is named by more than 40 tokens; some expert is named by exactly 40.
All inputs are finite; a program needn't handle non-finite values.
Results may differ from a plain program's by a relative error of at most 0.0045.
Values may be sent and summed in bfloat16 or wider, within the bound.
A program may use at most 192 MiB of HBM per device.

v0:
```python
import jax
import jax.numpy as jnp
from jax import lax
from jax.sharding import PartitionSpec as P

SPLIT = 4


def passed_along(x, axis, by):
    size = lax.axis_size(axis)
    return lax.ppermute(x, axis, [(i, (i + by) % size) for i in range(size)])


def normalize(values):
    floats = values.astype(jnp.float32)
    inv_rms = lax.rsqrt(jnp.mean(floats * floats, axis=-1, keepdims=True) + 1e-06)
    return (floats * inv_rms).astype(jnp.bfloat16)


def slot_table(routes, experts, capacity):
    flat_ids = routes.reshape(-1)
    onehot = (flat_ids[:, None] == jnp.arange(experts, dtype=jnp.int32)[None, :]).astype(jnp.int32)
    before = jnp.cumsum(onehot, axis=0) - onehot
    slot_idx = jnp.sum(before * onehot, axis=1).reshape(routes.shape)
    return routes * capacity + slot_idx


def local(tokens, expert_ids, gate_weights, w_gate, w_up, w_down):
    n_dev = lax.axis_size("expert")
    experts = n_dev // SPLIT
    local_tok = tokens[0]
    micro_count = local_tok.shape[0]
    tok_rows = local_tok.shape[1]
    feat_width = local_tok.shape[2]
    top_k = expert_ids.shape[-1]
    capacity = min(tok_rows, tok_rows * top_k * 5 // (4 * experts))
    slots_all = experts * capacity
    positions = jnp.arange(slots_all, dtype=jnp.int32)
    gate_mat = w_gate[0, 0]
    up_mat = w_up[0, 0]
    down_mat = w_down[0, 0]
    outgoing_all = []
    weighted_all = []
    for micro_idx in range(micro_count):
        normed = normalize(local_tok[micro_idx])
        target = slot_table(expert_ids[0, micro_idx], experts, capacity)
        matches = target[None, :, :] == positions[:, None, None]
        selector = jnp.sum(matches.astype(jnp.int32), axis=2).astype(jnp.bfloat16)
        dispatched = jnp.dot(selector, normed, preferred_element_type=jnp.float32).astype(
            jnp.bfloat16
        )
        dispatched = dispatched.reshape(experts, 1, capacity, feat_width)
        outgoing = jnp.broadcast_to(dispatched, (experts, SPLIT, capacity, feat_width))
        outgoing_all.append(outgoing.reshape(n_dev, capacity, feat_width))
        gate_vals = gate_weights[0, micro_idx]
        weighted = jnp.sum(jnp.where(matches, gate_vals[None, :, :], jnp.float32(0.0)), axis=2)
        weighted_all.append(jnp.transpose(weighted))
    results = []
    for micro_idx in range(micro_count):
        received = lax.all_to_all(
            outgoing_all[micro_idx], "expert", split_axis=0, concat_axis=0, tiled=True
        )
        in_shape = received.shape
        rows_in = received.reshape(-1, feat_width)
        gate_act = jnp.dot(rows_in, gate_mat, preferred_element_type=jnp.float32)
        up_act = jnp.dot(rows_in, up_mat, preferred_element_type=jnp.float32)
        hidden = (jax.nn.silu(gate_act) * up_act).astype(jnp.bfloat16)
        result = jnp.dot(hidden, down_mat, preferred_element_type=jnp.float32).astype(jnp.bfloat16)
        partials = result.reshape(in_shape)
        returned = lax.all_to_all(partials, "expert", split_axis=0, concat_axis=0, tiled=True)
        combined = returned.reshape(experts, SPLIT, capacity, feat_width).astype(jnp.float32)
        combined = jnp.sum(combined, axis=1).reshape(slots_all, feat_width)
        mixed_out = local_tok[micro_idx].astype(jnp.float32) + jnp.dot(
            weighted_all[micro_idx], combined, precision=lax.Precision.HIGHEST
        )
        results.append(passed_along(mixed_out.astype(jnp.bfloat16), "section", 1))
    passed = jnp.stack(results, axis=0)
    return passed[None]


def solution(mesh):
    return jax.shard_map(
        local,
        mesh=mesh,
        in_specs=(
            P("section", None, "expert", None),
            P("section", None, "expert", None),
            P("section", None, "expert", None),
            P("section", "expert", None, None),
            P("section", "expert", None, None),
            P("section", "expert", None, None),
        ),
        out_specs=P("section", None, "expert", None),
        check_vma=False,
    )
```

profile of v0, /device:TPU:12, one launch (start us, length us, event | category | flops | bytes accessed | tf_op | source)
XLA Modules:
  0.0 868.8 jit_solution(4525728620116955000)
XLA Ops:
  3.3 1.9 fusion.12
  5.3 2.0 convolution_convert_fusion.3
  7.3 4.7 broadcast_in_dim.51
  11.9 6.4 all-to-all-start
  18.4 2.2 convolution_convert_fusion.2
  20.6 196.7 %all-to-all-done = bf16[16,40,7168]{2,1,0:T(8,128)(2,1)} async-done(((bf16[16,40,7168]{2,1,0:T(8,128)(2,1)}), bf16[16,40,7168]{2,1,0:T(8,128)(2,1)}, u32[]{:S(2)}, u32[]{:S(2)}) %all-to-all-start) | async-done | bytes 9175072 | tf_op jit(solution)/shard_map/all_to_all | solution.py:60
  217.4 6.4 broadcast_in_dim.55
  223.7 5.1 all-to-all-start.2
  228.8 9.7 %fusion.10 = f32[640,512]{1,0:T(8,128)S(1)} fusion(bf16[640,7168]{1,0:T(8,128)(2,1)} %bitcast.6, bf16[1,1,7168,512]{3,2,1,0:T(8,128)(2,1)} %param.9), kind=kOutput, calls=%fused_computation.18 | convolution fusion | flops 4697620480 | bytes 17825792 | tf_op jit(solution)/shard_map/dot_general | solution.py:65
  238.5 10.9 %fusion.25 = bf16[640,512]{1,0:T(8,128)(2,1)S(1)} fusion(bf16[640,7168]{1,0:T(8,128)(2,1)} %bitcast.6, bf16[1,1,7168,512]{3,2,1,0:T(8,128)(2,1)} %param.10, f32[640,512]{1,0:T(8,128)S(1)} %fusion.10), kind=kOutput, calls=%fused_computation.32 | convolution fusion | flops 4699586560 | bytes 18481152 | tf_op jit(solution)/shard_map/dot_general | solution.py:66
  249.4 7.3 convolution_convert_fusion.1
  256.7 171.1 %all-to-all-done.2 = bf16[16,40,7168]{2,1,0:T(8,128)(2,1)} async-done(((bf16[16,40,7168]{2,1,0:T(8,128)(2,1)}), bf16[16,40,7168]{2,1,0:T(8,128)(2,1)}, u32[]{:S(2)}, u32[]{:S(2)}) %all-to-all-start.2) | async-done | bytes 9175072 | tf_op jit(solution)/shard_map/all_to_all | solution.py:60
  427.8 5.1 all-to-all-start.1
  432.9 9.7 %fusion.8 = f32[640,512]{1,0:T(8,128)S(1)} fusion(bf16[640,7168]{1,0:T(8,128)(2,1)} %bitcast.20, bf16[1,1,7168,512]{3,2,1,0:T(8,128)(2,1)} %param.9), kind=kOutput, calls=%fused_computation.16 | convolution fusion | flops 4697620480 | bytes 17825792 | tf_op jit(solution)/shard_map/dot_general | solution.py:65
  442.6 10.9 %fusion.22 = bf16[640,512]{1,0:T(8,128)(2,1)S(1)} fusion(bf16[640,7168]{1,0:T(8,128)(2,1)} %bitcast.20, bf16[1,1,7168,512]{3,2,1,0:T(8,128)(2,1)} %param.10, f32[640,512]{1,0:T(8,128)S(1)} %fusion.8), kind=kOutput, calls=%fused_computation.31 | convolution fusion | flops 4699586560 | bytes 18481152 | tf_op jit(solution)/shard_map/dot_general | solution.py:66
  453.5 7.3 convolution_convert_fusion
  460.8 171.2 %all-to-all-done.1 = bf16[16,40,7168]{2,1,0:T(8,128)(2,1)} async-done(((bf16[16,40,7168]{2,1,0:T(8,128)(2,1)}), bf16[16,40,7168]{2,1,0:T(8,128)(2,1)}, u32[]{:S(2)}, u32[]{:S(2)}) %all-to-all-start.1) | async-done | bytes 9175072 | tf_op jit(solution)/shard_map/all_to_all | solution.py:70
  632.0 5.2 all-to-all-start.3
  637.4 6.1 convert_reduce_fusion.1
  643.5 3.4 fusion
  648.4 187.8 %all-to-all-done.3 = bf16[16,40,7168]{2,1,0:T(8,128)(2,1)} async-done(((bf16[16,40,7168]{2,1,0:T(8,128)(2,1)}), bf16[16,40,7168]{2,1,0:T(8,128)(2,1)}, u32[]{:S(2)}, u32[]{:S(2)}) %all-to-all-start.3) | async-done | bytes 9175072 | tf_op jit(solution)/shard_map/all_to_all | solution.py:70
  836.2 6.1 convert_reduce_fusion
  842.3 2.5 fusion.1
  846.3 21.0 %collective-permute-done.1 = bf16[64,7168]{1,0:T(8,128)(2,1)S(1)} collective-permute-done((bf16[64,7168]{1,0:T(8,128)(2,1)S(1)}, bf16[64,7168]{1,0:T(8,128)(2,1)S(1)}, u32[]{:S(2)}, u32[]{:S(2)}) %collective-permute-start.1) | collective-permute-done | bytes 917536 | tf_op jit(solution)/shard_map/ppermute | solution.py:11
  (40 shorter events, 8.0 us)
Async XLA Ops:
  11.9 6.5 copy-start
  11.9 205.4 %all-to-all-start = ((bf16[16,40,7168]{2,1,0:T(8,128)(2,1)}), bf16[16,40,7168]{2,1,0:T(8,128)(2,1)}, u32[]{:S(2)}, u32[]{:S(2)}) async-start(bf16[16,40,7168]{2,1,0:T(8,128)(2,1)} %bitcast.81), calls=%async_computation | async-start | bytes 18350080 | tf_op jit(solution)/shard_map/all_to_all | solution.py:60
  223.7 204.1 %all-to-all-start.2 = ((bf16[16,40,7168]{2,1,0:T(8,128)(2,1)}), bf16[16,40,7168]{2,1,0:T(8,128)(2,1)}, u32[]{:S(2)}, u32[]{:S(2)}) async-start(bf16[16,40,7168]{2,1,0:T(8,128)(2,1)} %bitcast.82), calls=%async_computation.2 | async-start | bytes 18350080 | tf_op jit(solution)/shard_map/all_to_all | solution.py:60
  228.8 20.6 %slice-start = ((s8[7340032]{0:T(1024)(128)(4,1)}), s8[4194304]{0:T(1024)(128)(4,1)S(1)}, s32[]{:S(2)}) async-start(s8[7340032]{0:T(1024)(128)(4,1)} %bitcast.91), calls=%async_computation.4 | async-start | bytes 8388608
  238.5 10.9 %slice-start.1 = ((s8[7340032]{0:T(1024)(128)(4,1)}), s8[3145728]{0:T(1024)(128)(4,1)S(1)}, s32[]{:S(2)}) async-start(s8[7340032]{0:T(1024)(128)(4,1)} %bitcast.91), calls=%async_computation.5 | async-start | bytes 6291456
  427.8 204.1 %all-to-all-start.1 = ((bf16[16,40,7168]{2,1,0:T(8,128)(2,1)}), bf16[16,40,7168]{2,1,0:T(8,128)(2,1)}, u32[]{:S(2)}, u32[]{:S(2)}) async-start(bf16[16,40,7168]{2,1,0:T(8,128)(2,1)} %bitcast.86), calls=%async_computation.1 | async-start | bytes 18350080 | tf_op jit(solution)/shard_map/all_to_all | solution.py:70
  432.9 20.6 %slice-start.2 = ((s8[7340032]{0:T(1024)(128)(4,1)}), s8[4194304]{0:T(1024)(128)(4,1)S(1)}, s32[]{:S(2)}) async-start(s8[7340032]{0:T(1024)(128)(4,1)} %bitcast.93), calls=%async_computation.6 | async-start | bytes 8388608
  442.6 10.9 %slice-start.3 = ((s8[7340032]{0:T(1024)(128)(4,1)}), s8[3145728]{0:T(1024)(128)(4,1)S(1)}, s32[]{:S(2)}) async-start(s8[7340032]{0:T(1024)(128)(4,1)} %bitcast.93), calls=%async_computation.7 | async-start | bytes 6291456
  632.0 5.2 copy-start.1
  632.0 204.2 %all-to-all-start.3 = ((bf16[16,40,7168]{2,1,0:T(8,128)(2,1)}), bf16[16,40,7168]{2,1,0:T(8,128)(2,1)}, u32[]{:S(2)}, u32[]{:S(2)}) async-start(bf16[16,40,7168]{2,1,0:T(8,128)(2,1)} %bitcast.85), calls=%async_computation.3 | async-start | bytes 18350080 | tf_op jit(solution)/shard_map/all_to_all | solution.py:70
  646.9 199.5 %collective-permute-start = (bf16[64,7168]{1,0:T(8,128)(2,1)}, bf16[64,7168]{1,0:T(8,128)(2,1)S(1)}, u32[]{:S(2)}, u32[]{:S(2)}) collective-permute-start(bf16[64,7168]{1,0:T(8,128)(2,1)} %fusion), channel_id=1, source_target_pairs={{0,16},{16,0},{1,17},{17,1},{2,18},{18,2},{3,19},{19,3},{4,20},{20... | collective-permute-start | bytes 2752520 | tf_op jit(solution)/shard_map/ppermute | solution.py:11
  844.8 22.6 %collective-permute-start.1 = (bf16[64,7168]{1,0:T(8,128)(2,1)S(1)}, bf16[64,7168]{1,0:T(8,128)(2,1)S(1)}, u32[]{:S(2)}, u32[]{:S(2)}) collective-permute-start(bf16[64,7168]{1,0:T(8,128)(2,1)S(1)} %fusion.1), channel_id=1, source_target_pairs={{0,16},{16,0},{1,17},{17,1},{2,18},{18,2},{3,19},{19,3},{4,20},{20... | collective-permute-start | bytes 2752520 | tf_op jit(solution)/shard_map/ppermute | solution.py:11
where the time goes:
time: 869 us
  waiting for transfers between devices  748 us (86%)
  matrix products  65.8 us (8%)
  starting transfers between devices  24.7 us (3%)
  other arithmetic  17.4 us (2%)
  local copies, waits for them, and re-layouts  12.7 us (1%)
    all_to_all x2, waiting for transfers between devices, local(): lax.all_to_all(outgoing_all[micro_idx], 'expert', split_axis=0, concat_ax...  368 us
    all_to_all x2, waiting for transfers between devices, local(): lax.all_to_all(partials, 'expert', split_axis=0, concat_axis=0, tiled=True)  359 us
    dot_general x2, matrix products, local(): up_act = jnp.dot(rows_in, up_mat, preferred_element_type=jnp.float32)  21.7 us
    ppermute x2, waiting for transfers between devices, passed_along(): return lax.ppermute(x, axis, [(i, (i + by) % size) for i in range(size)])  21.1 us
    dot_general x2, matrix products, local(): gate_act = jnp.dot(rows_in, gate_mat, preferred_element_type=jnp.float32)  19.4 us
  transfers between devices with their start and end apart: 6, of which 5 were waited for; matrix products, arithmetic and copies ran while one was open for 9% of the time, Pallas kernels for 0%

commit v1 on v0

v1 whole, which is shorter than its diff:
```python
import functools

import jax
import jax.numpy as jnp
from jax import lax
from jax.experimental import pallas as pl
from jax.experimental.pallas import tpu as pltpu
from jax.sharding import PartitionSpec as P

SPLIT = 4
MESH = pl.DeviceIdType.MESH
VMEM_LIMIT = 60 * 1024 * 1024
Z_AHEAD = 2
Y_AHEAD = 2


def chunk_width(features):
    return max(w for w in range(128, 1025, 128) if features % w == 0)


def normalize(values):
    floats = values.astype(jnp.float32)
    inv_rms = lax.rsqrt(jnp.mean(floats * floats, axis=-1, keepdims=True) + 1e-06)
    return (floats * inv_rms).astype(jnp.bfloat16)


def places(experts):
    me = lax.axis_index("expert")
    own = lax.div(me, SPLIT)
    share = lax.rem(me, SPLIT)
    core = lax.rem(share, 2)
    chip = lax.div(share, 2)
    sibling = own * SPLIT + chip * 2 + (1 - core)
    across = own * SPLIT + (1 - chip) * 2 + core
    others = []
    for step in range(1, experts):
        other = lax.rem(own + step, experts)
        others.append((other, other * SPLIT + share))
    return own, core, chip, sibling, across, others


def remote(src, dst, send, recv, **where):
    return pltpu.make_async_remote_copy(
        src_ref=src, dst_ref=dst, send_sem=send, recv_sem=recv,
        device_id=where, device_id_type=MESH,
    )


def dispatch_kernel(
    experts, chunks, width,
    sel, normed, gate_hbm, up_hbm, hid,
    picked, rows, gate_w, up_w, gate_acc, up_acc,
    w_sem, z_s, z_r, y_s, y_r, a_s, a_r, b_s, b_r,
):
    own, core, chip, sibling, across, others = places(experts)
    units = sel.shape[0] // experts
    load_gate = pltpu.make_async_copy(gate_hbm, gate_w, w_sem.at[0])
    load_up = pltpu.make_async_copy(up_hbm, up_w, w_sem.at[1])
    load_gate.start()
    load_up.start()

    barrier = pltpu.get_barrier_semaphore()
    for partner in [sibling, across] + [dev for _, dev in others]:
        pl.semaphore_signal(barrier, inc=1, device_id={"expert": partner}, device_id_type=MESH)
    pl.semaphore_wait(barrier, experts + 1)

    gate_acc[...] = jnp.zeros_like(gate_acc)
    up_acc[...] = jnp.zeros_like(up_acc)

    def z_copy(c, n):
        other, dev = others[n]
        return remote(picked.at[c, other], rows.at[c, core, chip, own], z_s.at[c, n], z_r.at[c, n], expert=dev)

    def y_copy(c):
        slab = rows.at[c, core, chip]
        return remote(slab, slab, y_s.at[c], y_r.at[c], expert=across)

    def a_copy(c):
        slab = rows.at[c, core, chip]
        return remote(slab, slab, a_s.at[c], a_r.at[c], expert=sibling)

    def b_copy(c):
        slab = rows.at[c, core, 1 - chip]
        return remote(slab, slab, b_s.at[c], b_r.at[c], expert=sibling)

    def multiply(c, co, yo):
        lhs = rows[c, co, yo].reshape(experts * units, width)
        at = pl.ds(pl.multiple_of(c * width, width), width)
        gate_acc[co, yo] += jnp.dot(lhs, gate_w[at, :], preferred_element_type=jnp.float32)
        up_acc[co, yo] += jnp.dot(lhs, up_w[at, :], preferred_element_type=jnp.float32)

    @pl.loop(0, chunks + Z_AHEAD + Y_AHEAD + 1)
    def _(t):
        @pl.when(t < chunks)
        def _():
            at = pl.ds(pl.multiple_of(t * width, width), width)
            block = jnp.dot(sel[...], normed[:, at], preferred_element_type=jnp.float32)
            picked[t] = block.astype(jnp.bfloat16).reshape(experts, units, width)
            for n in range(experts - 1):
                z_copy(t, n).start()
            rows[t, core, chip, own] = picked[t, own]

        c1 = t - Z_AHEAD

        @pl.when((c1 >= 0) & (c1 < chunks))
        def _():
            for n in range(experts - 1):
                z_copy(c1, n).wait_recv()
            y_copy(c1).start()
            a_copy(c1).start()

        c2 = c1 - Y_AHEAD

        @pl.when((c2 >= 0) & (c2 < chunks))
        def _():
            y_copy(c2).wait_recv()
            b_copy(c2).start()

        @pl.when(c2 == 0)
        def _():
            load_gate.wait()
            load_up.wait()

        @pl.when((c2 >= 0) & (c2 < chunks))
        def _():
            @pl.loop(0, 2)
            def _(yo):
                multiply(c2, core, yo)

        c3 = c2 - 1

        @pl.when((c3 >= 0) & (c3 < chunks))
        def _():
            a_copy(c3).wait_recv()
            b_copy(c3).wait_recv()

            @pl.loop(0, 2)
            def _(yo):
                multiply(c3, 1 - core, yo)

    @pl.loop(0, chunks)
    def _(c):
        for n in range(experts - 1):
            z_copy(c, n).wait_send()
        y_copy(c).wait_send()
        a_copy(c).wait_send()
        b_copy(c).wait_send()

    @pl.loop(0, 4)
    def _(k):
        co, yo = lax.div(k, 2), lax.rem(k, 2)
        gate = gate_acc[co, yo]
        hid[co, yo] = (gate / (1.0 + jnp.exp(-gate)) * up_acc[co, yo]).astype(jnp.bfloat16)


def return_kernel(
    experts, chunks, width,
    hid, down_hbm, mix_hi, mix_lo, tok, out,
    part, from_core, from_chip, back, staged, down_w,
    w_sem, a_s, a_r, y_s, y_r, z_s, z_r, o_s, o_r,
):
    own, core, chip, sibling, across, others = places(experts)
    units = back.shape[2]
    section = lax.axis_index("section")
    n_sections = lax.axis_size("section")
    after = lax.rem(section + 1, n_sections)
    before = lax.rem(section + n_sections - 1, n_sections)
    load = pltpu.make_async_copy(down_hbm, down_w, w_sem.at[0])
    load.start()

    barrier = pltpu.get_barrier_semaphore()
    for partner in [sibling, across] + [dev for _, dev in others]:
        pl.semaphore_signal(barrier, inc=1, device_id={"expert": partner}, device_id_type=MESH)
    pl.semaphore_signal(barrier, inc=1, device_id={"section": before}, device_id_type=MESH)
    pl.semaphore_wait(barrier, experts + 2)
    load.wait()

    def columns(c):
        return pl.ds(pl.multiple_of(c * width, width), width)

    def a_copy(c):
        return remote(part.at[c, 1 - core], from_core.at[c], a_s.at[c], a_r.at[c], expert=sibling)

    def y_copy(c):
        return remote(part.at[c, core, 1 - chip], from_chip.at[c], y_s.at[c], y_r.at[c], expert=across)

    def z_copy(c, n):
        other, dev = others[n]
        return remote(part.at[c, core, chip, other], back.at[c, own], z_s.at[c, n], z_r.at[c, n], expert=dev)

    def o_copy(c):
        return remote(staged.at[c], out.at[:, columns(c)], o_s.at[c], o_r.at[c], section=after)

    def multiply(c, co, yo):
        block = jnp.dot(hid[co, yo].reshape(experts * units, hid.shape[-1]), down_w[:, columns(c)], preferred_element_type=jnp.float32)
        part[c, co, yo] = block.astype(jnp.bfloat16).reshape(experts, units, width)

    @pl.loop(0, chunks + 2 + Y_AHEAD + Z_AHEAD)
    def _(t):
        @pl.when(t < chunks)
        def _():
            @pl.loop(0, 2)
            def _(yo):
                multiply(t, 1 - core, yo)

            a_copy(t).start()

            @pl.loop(0, 2)
            def _(yo):
                multiply(t, core, yo)

        c1 = t - 1

        @pl.when((c1 >= 0) & (c1 < chunks))
        def _():
            a_copy(c1).wait_recv()

            @pl.loop(0, experts)
            def _(e):
                total = part[c1, core, 1 - chip, e].astype(jnp.float32) + from_core[c1, 1 - chip, e].astype(jnp.float32)
                part[c1, core, 1 - chip, e] = total.astype(jnp.bfloat16)

            y_copy(c1).start()

        c2 = c1 - Y_AHEAD

        @pl.when((c2 >= 0) & (c2 < chunks))
        def _():
            y_copy(c2).wait_recv()

            @pl.loop(0, experts)
            def _(e):
                total = part[c2, core, chip, e].astype(jnp.float32) + from_core[c2, chip, e].astype(jnp.float32)
                total = total + from_chip[c2, e].astype(jnp.float32)
                part[c2, core, chip, e] = total.astype(jnp.bfloat16)

            for n in range(experts - 1):
                z_copy(c2, n).start()
            back[c2, own] = part[c2, core, chip, own]

        c3 = c2 - Z_AHEAD

        @pl.when((c3 >= 0) & (c3 < chunks))
        def _():
            for n in range(experts - 1):
                z_copy(c3, n).wait_recv()
            terms = back[c3].reshape(experts * units, width)
            total = jnp.dot(mix_hi[...], terms, preferred_element_type=jnp.float32)
            total += jnp.dot(mix_lo[...], terms, preferred_element_type=jnp.float32)
            total += tok[:, columns(c3)].astype(jnp.float32)
            staged[c3] = total.astype(jnp.bfloat16)
            o_copy(c3).start()

    @pl.loop(0, chunks)
    def _(c):
        a_copy(c).wait_send()
        y_copy(c).wait_send()
        for n in range(experts - 1):
            z_copy(c, n).wait_send()
        o_copy(c).wait()


def local(tokens, expert_ids, gate_weights, w_gate, w_up, w_down):
    n_dev = lax.axis_size("expert")
    experts = n_dev // SPLIT
    local_tok = tokens[0]
    micro_count, tok_rows, features = local_tok.shape
    top_k = expert_ids.shape[-1]
    hidden = w_gate.shape[-1]
    capacity = min(tok_rows, tok_rows * top_k * 5 // (4 * experts))
    units = -(-micro_count * capacity // 16) * 16
    width = chunk_width(features)
    chunks = features // width
    all_tok = micro_count * tok_rows

    ids = expert_ids[0].reshape(micro_count, tok_rows * top_k)
    order = jnp.arange(tok_rows * top_k, dtype=jnp.int32)
    same = (ids[:, :, None] == ids[:, None, :]) & (order[None, :] < order[:, None])[None]
    slot = jnp.sum(same.astype(jnp.int32), axis=2)
    micro = jnp.arange(micro_count, dtype=jnp.int32)[:, None]
    target = (ids * units + micro * capacity + slot).reshape(all_tok, top_k)
    positions = jnp.arange(experts * units, dtype=jnp.int32)
    sel = jnp.sum((positions[:, None, None] == target[None]).astype(jnp.float32), axis=2).astype(jnp.bfloat16)
    gates = gate_weights[0].reshape(all_tok, top_k)
    mix = jnp.sum(jnp.where(target[:, :, None] == positions[None, None, :], gates[:, :, None], 0.0), axis=1)
    mix_hi = lax.reduce_precision(mix, 8, 7)
    mix_lo = (mix - mix_hi).astype(jnp.bfloat16)
    mix_hi = mix_hi.astype(jnp.bfloat16)

    flat_tok = local_tok.reshape(all_tok, features)
    normed = normalize(flat_tok)

    vmem = pl.BlockSpec(memory_space=pltpu.VMEM)
    anywhere = pl.BlockSpec(memory_space=pl.ANY)
    dma = pltpu.SemaphoreType.DMA
    bf16 = jnp.bfloat16
    macs = n_dev * units * features * hidden
    hid = pl.pallas_call(
        functools.partial(dispatch_kernel, experts, chunks, width),
        out_shape=jax.ShapeDtypeStruct((2, 2, experts * units, hidden), bf16),
        in_specs=[vmem, vmem, anywhere, anywhere],
        out_specs=vmem,
        scratch_shapes=[
            pltpu.VMEM((chunks, experts, units, width), bf16),
            pltpu.VMEM((chunks, 2, 2, experts, units, width), bf16),
            pltpu.VMEM((features, hidden), bf16),
            pltpu.VMEM((features, hidden), bf16),
            pltpu.VMEM((2, 2, experts * units, hidden), jnp.float32),
            pltpu.VMEM((2, 2, experts * units, hidden), jnp.float32),
            dma((2,)),
            dma((chunks, experts - 1)), dma((chunks, experts - 1)),
            dma((chunks,)), dma((chunks,)),
            dma((chunks,)), dma((chunks,)),
            dma((chunks,)), dma((chunks,)),
        ],
        compiler_params=pltpu.CompilerParams(
            collective_id=0, has_side_effects=True, vmem_limit_bytes=VMEM_LIMIT
        ),
        cost_estimate=pl.CostEstimate(flops=4 * macs, bytes_accessed=4 * features * hidden, transcendentals=0),
        name="dispatch",
    )(sel, normed, w_gate[0, 0], w_up[0, 0])
    passed = pl.pallas_call(
        functools.partial(return_kernel, experts, chunks, width),
        out_shape=jax.ShapeDtypeStruct((all_tok, features), bf16),
        in_specs=[vmem, anywhere, vmem, vmem, vmem],
        out_specs=anywhere,
        scratch_shapes=[
            pltpu.VMEM((chunks, 2, 2, experts, units, width), bf16),
            pltpu.VMEM((chunks, 2, experts, units, width), bf16),
            pltpu.VMEM((chunks, experts, units, width), bf16),
            pltpu.VMEM((chunks, experts, units, width), bf16),
            pltpu.VMEM((chunks, all_tok, width), bf16),
            pltpu.VMEM((hidden, features), bf16),
            dma((1,)),
            dma((chunks,)), dma((chunks,)),
            dma((chunks,)), dma((chunks,)),
            dma((chunks, experts - 1)), dma((chunks, experts - 1)),
            dma((chunks,)), dma((chunks,)),
        ],
        compiler_params=pltpu.CompilerParams(
            collective_id=1, has_side_effects=True, vmem_limit_bytes=VMEM_LIMIT
        ),
        cost_estimate=pl.CostEstimate(flops=2 * macs, bytes_accessed=2 * features * hidden, transcendentals=0),
        name="combine",
    )(hid, w_down[0, 0], mix_hi, mix_lo, flat_tok)
    return passed.reshape(1, micro_count, tok_rows, features)


def solution(mesh):
    return jax.shard_map(
        local,
        mesh=mesh,
        in_specs=(
            P("section", None, "expert", None),
            P("section", None, "expert", None),
            P("section", None, "expert", None),
            P("section", "expert", None, None),
            P("section", "expert", None, None),
            P("section", "expert", None, None),
        ),
        out_specs=P("section", None, "expert", None),
        check_vma=False,
    )
```

time: 869 us -> 289 us (0.33)
  waiting for transfers between devices: 748 us -> 0 us
  Pallas kernels: 0 us -> 276 us
  matrix products: 65.8 us -> 0 us
  starting transfers between devices: 24.7 us -> 0 us
  other arithmetic: 17.4 us -> 6.14 us
    all_to_all x4 -> x0, waiting for transfers between devices: 727 us -> none  [the longest x2 368 us: local(): lax.all_to_all(outgoing_all[micro_idx], 'expert', split_axis=0, concat_ax...]
    pallas_call x0 -> x2, Pallas kernels: none -> 276 us  [the longest x1 140 us: local(): pl.pallas_call(functools.partial(dispatch_kernel, experts, chunks, width)...]
    dot_general x10 -> x0, matrix products: 65.8 us -> none  [the longest x2 21.7 us: local(): up_act = jnp.dot(rows_in, up_mat, preferred_element_type=jnp.float32)]
    all_to_all x4 -> x0, starting transfers between devices: 21.7 us -> none  [the longest x2 11.4 us: local(): lax.all_to_all(outgoing_all[micro_idx], 'expert', split_axis=0, concat_ax...]
    ppermute x2 -> x0, waiting for transfers between devices: 21.1 us -> none  [passed_along(): return lax.ppermute(x, axis, [(i, (i + by) % size) for i in range(size)])]
    reduce_sum x8 -> x3, other arithmetic: 12.9 us -> 0.91 us  [the longest x1 0.69 us: local(): jnp.sum((positions[:, None, None] == target[None]).astype(jnp.float32), a...]
    broadcast_in_dim x3 -> x1, local copies, waits for them, and re-layouts: 11 us -> 0.08 us  [local(): jnp.where(target[:, :, None] == positions[None, None, :], gates[:, :, Non...]
  transfers between devices with their start and end apart: 6 -> 0, of which waited for: 5 -> 0; matrix products, arithmetic and copies ran while one was open for 9% -> 0% of each run, Pallas kernels for 0% -> 0%
where the time goes in v1:
time: 289 us; the launch traced here: 288 us
  Pallas kernels  276 us (96%)
  other arithmetic  6.14 us (2%)
  local copies, waits for them, and re-layouts  5.34 us (2%)
    pallas_call x1, Pallas kernels, local(): pl.pallas_call(functools.partial(dispatch_kernel, experts, chunks, width)...  140 us
    pallas_call x1, Pallas kernels, local(): pl.pallas_call(functools.partial(return_kernel, experts, chunks, width),...  136 us

profile of v1, /device:TPU:12, one launch (start us, length us, event | category | flops | bytes accessed | tf_op | source)
XLA Modules:
  0.0 287.7 jit_solution(5416110445431280308)
XLA Ops:
  0.0 0.0 copy-start
  0.0 0.1 add.43
  0.1 0.1 add.44
  0.2 2.1 multiply_reduce_fusion
  2.2 0.1 rsqrt.12
  2.3 0.7 copy.23
  3.0 0.1 broadcast_in_dim.14
  3.1 0.7 broadcast_multiply_fusion
  3.8 0.1 mul.39
  3.9 0.8 copy.21
  4.7 0.1 eq.42
  4.8 0.2 convert_reduce_fusion.1
  5.0 0.1 reduce_sum.39
  5.2 0.1 copy.22
  5.2 0.7 convert_reduce_fusion.sel
  6.0 0.1 copy.25
  6.1 0.1 copy.24
  6.2 0.7 subtract_convert_fusion
  7.0 0.0 copy-done
  7.0 1.7 multiply_convert_fusion.normed
  8.7 140.4 %dispatch.1.hid = bf16[2,2,320,512]{3,2,1,0:T(8,128)(2,1)} custom-call(bf16[320,128]{1,0:T(8,128)(2,1)} %convert_reduce_fusion.sel, bf16[128,7168]{1,0:T(8,128)(2,1)} %multiply_convert_fusion.normed, bf16[7168,512]{1,0:T(8,128)(2,1)} %bitcast.14, bf16[7168,512]{1,0:T(8,128)(2,1)} %bitcast.15), custom_call_target="tpu_custom_call" | custom-call | flops 18790481920 | bytes 14680064 | tf_op jit(solution)/shard_map/dispatch/pallas_call | solution.py:298
  149.1 135.8 %combine.1 = bf16[128,7168]{1,0:T(8,128)(2,1)} custom-call(bf16[2,2,320,512]{3,2,1,0:T(8,128)(2,1)} %dispatch.1.hid, bf16[512,7168]{1,0:T(8,128)(2,1)} %bitcast.16, bf16[128,320]{1,0:T(8,128)(2,1)} %get-tuple-element.6.mix_hi, bf16[128,320]{1,0:T(8,128)(2,1)} %get-tuple-element.5.mix_lo, bf16[128,7168]{1,0:T(8,128)(2,1)} %bitcast.12), custom_call_target="tpu_custom_call" | custom-call | flops 9395240960 | bytes 7340032 | tf_op jit(solution)/shard_map/combine/pallas_call | solution.py:322
  284.9 2.8 copy.28
  (7 shorter events, 0.1 us)
Async XLA Ops:
  0.0 7.0 %copy-start = (bf16[1,2,64,7168]{3,2,1,0:T(8,128)(2,1)S(1)}, bf16[1,2,64,7168]{3,2,1,0:T(8,128)(2,1)}, u32[]{:S(2)}) copy-start(bf16[1,2,64,7168]{3,2,1,0:T(8,128)(2,1)} %param.6) | copy-start | bytes 5505028

commit v2 on v1

--- a/solution.py
+++ b/solution.py
@@ -12,16 +12,11 @@
 VMEM_LIMIT = 60 * 1024 * 1024
 Z_AHEAD = 2
 Y_AHEAD = 2
+OWN_LATER = 2
 
 
 def chunk_width(features):
-    return max(w for w in range(128, 1025, 128) if features % w == 0)
-
-
-def normalize(values):
-    floats = values.astype(jnp.float32)
-    inv_rms = lax.rsqrt(jnp.mean(floats * floats, axis=-1, keepdims=True) + 1e-06)
-    return (floats * inv_rms).astype(jnp.bfloat16)
+    return max(w for w in range(128, 257, 128) if features % w == 0)
 
 
 def places(experts):
@@ -48,12 +43,16 @@
 
 def dispatch_kernel(
     experts, chunks, width,
-    sel, normed, gate_hbm, up_hbm, hid,
-    picked, rows, gate_w, up_w, gate_acc, up_acc,
+    target, tok, gate_hbm, up_hbm, hid,
+    sel, inv_rms, picked, rows, gate_w, up_w, gate_acc, up_acc,
     w_sem, z_s, z_r, y_s, y_r, a_s, a_r, b_s, b_r,
 ):
     own, core, chip, sibling, across, others = places(experts)
     units = sel.shape[0] // experts
+
+    def columns(c):
+        return pl.ds(pl.multiple_of(c * width, width), width)
+
     load_gate = pltpu.make_async_copy(gate_hbm, gate_w, w_sem.at[0])
     load_up = pltpu.make_async_copy(up_hbm, up_w, w_sem.at[1])
     load_gate.start()
@@ -62,8 +61,22 @@
     barrier = pltpu.get_barrier_semaphore()
     for partner in [sibling, across] + [dev for _, dev in others]:
         pl.semaphore_signal(barrier, inc=1, device_id={"expert": partner}, device_id_type=MESH)
+
+    places_in = lax.broadcasted_iota(jnp.int32, sel.shape, 0)
+    hits = jnp.zeros(sel.shape, jnp.float32)
+    for k in range(target.shape[0]):
+        hits += jnp.where(places_in == target[k : k + 1, :], 1.0, 0.0)
+    sel[...] = hits.astype(jnp.bfloat16)
+
+    def add_squares(c, total):
+        part = tok[:, columns(c)].astype(jnp.float32)
+        return total + jnp.sum(part * part, axis=1, keepdims=True)
+
+    squares = lax.fori_loop(0, chunks, add_squares, jnp.zeros((tok.shape[0], 1), jnp.float32))
+    mean = squares / (chunks * width)
+    inv_rms[...] = jnp.broadcast_to(lax.rsqrt(mean + 1e-06), inv_rms.shape)
+
     pl.semaphore_wait(barrier, experts + 1)
-
     gate_acc[...] = jnp.zeros_like(gate_acc)
     up_acc[...] = jnp.zeros_like(up_acc)
 
@@ -71,9 +84,10 @@
         other, dev = others[n]
         return remote(picked.at[c, other], rows.at[c, core, chip, own], z_s.at[c, n], z_r.at[c, n], expert=dev)
 
-    def y_copy(c):
-        slab = rows.at[c, core, chip]
-        return remote(slab, slab, y_s.at[c], y_r.at[c], expert=across)
+    def y_copy(c, n):
+        home = own if n == experts - 1 else others[experts - 2 - n][0]
+        block = rows.at[c, core, chip, home]
+        return remote(block, block, y_s.at[c, n], y_r.at[c, n], expert=across)
 
     def a_copy(c):
         slab = rows.at[c, core, chip]
@@ -85,20 +99,20 @@
 
     def multiply(c, co, yo):
         lhs = rows[c, co, yo].reshape(experts * units, width)
-        at = pl.ds(pl.multiple_of(c * width, width), width)
-        gate_acc[co, yo] += jnp.dot(lhs, gate_w[at, :], preferred_element_type=jnp.float32)
-        up_acc[co, yo] += jnp.dot(lhs, up_w[at, :], preferred_element_type=jnp.float32)
+        gate_acc[co, yo] += jnp.dot(lhs, gate_w[columns(c), :], preferred_element_type=jnp.float32)
+        up_acc[co, yo] += jnp.dot(lhs, up_w[columns(c), :], preferred_element_type=jnp.float32)
 
     @pl.loop(0, chunks + Z_AHEAD + Y_AHEAD + 1)
     def _(t):
         @pl.when(t < chunks)
         def _():
-            at = pl.ds(pl.multiple_of(t * width, width), width)
-            block = jnp.dot(sel[...], normed[:, at], preferred_element_type=jnp.float32)
+            normed = (tok[:, columns(t)].astype(jnp.float32) * inv_rms[:, :1]).astype(jnp.bfloat16)
+            block = jnp.dot(sel[...], normed, preferred_element_type=jnp.float32)
             picked[t] = block.astype(jnp.bfloat16).reshape(experts, units, width)
             for n in range(experts - 1):
                 z_copy(t, n).start()
             rows[t, core, chip, own] = picked[t, own]
+            y_copy(t, experts - 1).start()
 
         c1 = t - Z_AHEAD
 
@@ -106,14 +120,15 @@
         def _():
             for n in range(experts - 1):
                 z_copy(c1, n).wait_recv()
-            y_copy(c1).start()
+                y_copy(c1, n).start()
             a_copy(c1).start()
 
         c2 = c1 - Y_AHEAD
 
         @pl.when((c2 >= 0) & (c2 < chunks))
         def _():
-            y_copy(c2).wait_recv()
+            for n in range(experts):
+                y_copy(c2, n).wait_recv()
             b_copy(c2).start()
 
         @pl.when(c2 == 0)
@@ -142,7 +157,8 @@
     def _(c):
         for n in range(experts - 1):
             z_copy(c, n).wait_send()
-        y_copy(c).wait_send()
+        for n in range(experts):
+            y_copy(c, n).wait_send()
         a_copy(c).wait_send()
         b_copy(c).wait_send()
 
@@ -155,8 +171,8 @@
 
 def return_kernel(
     experts, chunks, width,
-    hid, down_hbm, mix_hi, mix_lo, tok, out,
-    part, from_core, from_chip, back, staged, down_w,
+    hid, down_hbm, target, gates, tok, out,
+    mix_hi, mix_lo, part, from_core, from_chip, back, staged, down_w,
     w_sem, a_s, a_r, y_s, y_r, z_s, z_r, o_s, o_r,
 ):
     own, core, chip, sibling, across, others = places(experts)
@@ -165,24 +181,42 @@
     n_sections = lax.axis_size("section")
     after = lax.rem(section + 1, n_sections)
     before = lax.rem(section + n_sections - 1, n_sections)
-    load = pltpu.make_async_copy(down_hbm, down_w, w_sem.at[0])
-    load.start()
+
+    def columns(c):
+        return pl.ds(pl.multiple_of(c * width, width), width)
+
+    def load(c):
+        return pltpu.make_async_copy(down_hbm.at[:, columns(c)], down_w.at[:, columns(c)], w_sem.at[c])
+
+    @pl.loop(0, chunks)
+    def _(c):
+        load(c).start()
 
     barrier = pltpu.get_barrier_semaphore()
     for partner in [sibling, across] + [dev for _, dev in others]:
         pl.semaphore_signal(barrier, inc=1, device_id={"expert": partner}, device_id_type=MESH)
     pl.semaphore_signal(barrier, inc=1, device_id={"section": before}, device_id_type=MESH)
+
+    places_in = lax.broadcasted_iota(jnp.int32, mix_hi.shape, 1)
+    mix = jnp.zeros(mix_hi.shape, jnp.float32)
+    for k in range(target.shape[1]):
+        mix += jnp.where(places_in == target[:, k : k + 1], gates[:, k : k + 1], 0.0)
+    high = mix.astype(jnp.bfloat16)
+    mix_hi[...] = high
+    mix_lo[...] = (mix - high.astype(jnp.float32)).astype(jnp.bfloat16)
+
     pl.semaphore_wait(barrier, experts + 2)
-    load.wait()
-
-    def columns(c):
-        return pl.ds(pl.multiple_of(c * width, width), width)
 
     def a_copy(c):
         return remote(part.at[c, 1 - core], from_core.at[c], a_s.at[c], a_r.at[c], expert=sibling)
 
-    def y_copy(c):
-        return remote(part.at[c, core, 1 - chip], from_chip.at[c], y_s.at[c], y_r.at[c], expert=across)
+    def y_copy(c, n):
+        home = own if n == experts - 1 else others[n][0]
+        return remote(part.at[c, core, 1 - chip, home], from_chip.at[c, home], y_s.at[c, n], y_r.at[c, n], expert=across)
+
+    def whole(c, home):
+        total = part[c, core, chip, home].astype(jnp.float32) + from_core[c, chip, home].astype(jnp.float32)
+        return (total + from_chip[c, home].astype(jnp.float32)).astype(jnp.bfloat16)
 
     def z_copy(c, n):
         other, dev = others[n]
@@ -199,6 +233,8 @@
     def _(t):
         @pl.when(t < chunks)
         def _():
+            load(t).wait()
+
             @pl.loop(0, 2)
             def _(yo):
                 multiply(t, 1 - core, yo)
@@ -220,28 +256,31 @@
                 total = part[c1, core, 1 - chip, e].astype(jnp.float32) + from_core[c1, 1 - chip, e].astype(jnp.float32)
                 part[c1, core, 1 - chip, e] = total.astype(jnp.bfloat16)
 
-            y_copy(c1).start()
+            for n in range(experts - 1):
+                y_copy(c1, n).start()
+
+        late = c1 - OWN_LATER
+
+        @pl.when((late >= 0) & (late < chunks))
+        def _():
+            y_copy(late, experts - 1).start()
 
         c2 = c1 - Y_AHEAD
 
         @pl.when((c2 >= 0) & (c2 < chunks))
         def _():
-            y_copy(c2).wait_recv()
-
-            @pl.loop(0, experts)
-            def _(e):
-                total = part[c2, core, chip, e].astype(jnp.float32) + from_core[c2, chip, e].astype(jnp.float32)
-                total = total + from_chip[c2, e].astype(jnp.float32)
-                part[c2, core, chip, e] = total.astype(jnp.bfloat16)
-
-            for n in range(experts - 1):
+            for n in range(experts - 1):
+                y_copy(c2, n).wait_recv()
+                other = others[n][0]
+                part[c2, core, chip, other] = whole(c2, other)
                 z_copy(c2, n).start()
-            back[c2, own] = part[c2, core, chip, own]
 
         c3 = c2 - Z_AHEAD
 
         @pl.when((c3 >= 0) & (c3 < chunks))
         def _():
+            y_copy(c3, experts - 1).wait_recv()
+            back[c3, own] = whole(c3, own)
             for n in range(experts - 1):
                 z_copy(c3, n).wait_recv()
             terms = back[c3].reshape(experts * units, width)
@@ -254,7 +293,8 @@
     @pl.loop(0, chunks)
     def _(c):
         a_copy(c).wait_send()
-        y_copy(c).wait_send()
+        for n in range(experts):
+            y_copy(c, n).wait_send()
         for n in range(experts - 1):
             z_copy(c, n).wait_send()
         o_copy(c).wait()
@@ -279,16 +319,8 @@
     slot = jnp.sum(same.astype(jnp.int32), axis=2)
     micro = jnp.arange(micro_count, dtype=jnp.int32)[:, None]
     target = (ids * units + micro * capacity + slot).reshape(all_tok, top_k)
-    positions = jnp.arange(experts * units, dtype=jnp.int32)
-    sel = jnp.sum((positions[:, None, None] == target[None]).astype(jnp.float32), axis=2).astype(jnp.bfloat16)
     gates = gate_weights[0].reshape(all_tok, top_k)
-    mix = jnp.sum(jnp.where(target[:, :, None] == positions[None, None, :], gates[:, :, None], 0.0), axis=1)
-    mix_hi = lax.reduce_precision(mix, 8, 7)
-    mix_lo = (mix - mix_hi).astype(jnp.bfloat16)
-    mix_hi = mix_hi.astype(jnp.bfloat16)
-
     flat_tok = local_tok.reshape(all_tok, features)
-    normed = normalize(flat_tok)
 
     vmem = pl.BlockSpec(memory_space=pltpu.VMEM)
     anywhere = pl.BlockSpec(memory_space=pl.ANY)
@@ -301,6 +333,8 @@
         in_specs=[vmem, vmem, anywhere, anywhere],
         out_specs=vmem,
         scratch_shapes=[
+            pltpu.VMEM((experts * units, all_tok), bf16),
+            pltpu.VMEM((all_tok, 128), jnp.float32),
             pltpu.VMEM((chunks, experts, units, width), bf16),
             pltpu.VMEM((chunks, 2, 2, experts, units, width), bf16),
             pltpu.VMEM((features, hidden), bf16),
@@ -309,7 +343,7 @@
             pltpu.VMEM((2, 2, experts * units, hidden), jnp.float32),
             dma((2,)),
             dma((chunks, experts - 1)), dma((chunks, experts - 1)),
-            dma((chunks,)), dma((chunks,)),
+            dma((chunks, experts)), dma((chunks, experts)),
             dma((chunks,)), dma((chunks,)),
             dma((chunks,)), dma((chunks,)),
         ],
@@ -318,22 +352,24 @@
         ),
         cost_estimate=pl.CostEstimate(flops=4 * macs, bytes_accessed=4 * features * hidden, transcendentals=0),
         name="dispatch",
-    )(sel, normed, w_gate[0, 0], w_up[0, 0])
+    )(target.T, flat_tok, w_gate[0, 0], w_up[0, 0])
     passed = pl.pallas_call(
         functools.partial(return_kernel, experts, chunks, width),
         out_shape=jax.ShapeDtypeStruct((all_tok, features), bf16),
         in_specs=[vmem, anywhere, vmem, vmem, vmem],
         out_specs=anywhere,
         scratch_shapes=[
+            pltpu.VMEM((all_tok, experts * units), bf16),
+            pltpu.VMEM((all_tok, experts * units), bf16),
             pltpu.VMEM((chunks, 2, 2, experts, units, width), bf16),
             pltpu.VMEM((chunks, 2, experts, units, width), bf16),
             pltpu.VMEM((chunks, experts, units, width), bf16),
             pltpu.VMEM((chunks, experts, units, width), bf16),
             pltpu.VMEM((chunks, all_tok, width), bf16),
             pltpu.VMEM((hidden, features), bf16),
-            dma((1,)),
+            dma((chunks,)),
             dma((chunks,)), dma((chunks,)),
-            dma((chunks,)), dma((chunks,)),
+            dma((chunks, experts)), dma((chunks, experts)),
             dma((chunks, experts - 1)), dma((chunks, experts - 1)),
             dma((chunks,)), dma((chunks,)),
         ],
@@ -342,7 +378,7 @@
         ),
         cost_estimate=pl.CostEstimate(flops=2 * macs, bytes_accessed=2 * features * hidden, transcendentals=0),
         name="combine",
-    )(hid, w_down[0, 0], mix_hi, mix_lo, flat_tok)
+    )(hid, w_down[0, 0], target, gates, flat_tok)
     return passed.reshape(1, micro_count, tok_rows, features)
 
 

time: 289 us -> 247 us (0.85)
  Pallas kernels: 276 us -> 238 us
  other arithmetic: 6.14 us -> 0.97 us
    pallas_call x1, Pallas kernels: 140 us -> 120 us  [local(): pl.pallas_call(functools.partial(dispatch_kernel, experts, chunks, width)...]
    pallas_call x1, Pallas kernels: 136 us -> 118 us  [local(): pl.pallas_call(functools.partial(return_kernel, experts, chunks, width),...]
where the time goes in v2:
time: 247 us; the launch traced here: 245 us
  Pallas kernels  238 us (96%)
  local copies, waits for them, and re-layouts  6.25 us (3%)
    pallas_call x1, Pallas kernels, local(): pl.pallas_call(functools.partial(dispatch_kernel, experts, chunks, width)...  120 us
    pallas_call x1, Pallas kernels, local(): pl.pallas_call(functools.partial(return_kernel, experts, chunks, width),...  118 us
    unnamed x5, local copies, waits for them, and re-layouts  5.04 us

profile of v2, /device:TPU:12, one launch (start us, length us, event | category | flops | bytes accessed | tf_op | source)
XLA Modules:
  0.0 245.2 jit_solution(4885561530879193409)
XLA Ops:
  0.0 0.1 add.17
  0.1 0.1 add.18
  0.2 0.7 broadcast_multiply_fusion
  0.9 0.1 copy.14
  1.0 1.4 copy.17
  2.4 0.8 copy.15
  3.2 0.1 eq.15
  3.3 0.2 convert_reduce_fusion
  3.5 0.1 reduce_sum.12
  3.6 0.1 fusion.target
  3.7 0.0 copy-start
  3.7 0.7 copy.16.target
  4.4 119.8 %dispatch.1.hid = bf16[2,2,320,512]{3,2,1,0:T(8,128)(2,1)} custom-call(s32[2,128]{1,0:T(2,128)} %copy.16.target, bf16[128,7168]{1,0:T(8,128)(2,1)} %bitcast.19, bf16[7168,512]{1,0:T(8,128)(2,1)} %bitcast.16, bf16[7168,512]{1,0:T(8,128)(2,1)} %bitcast.17), custom_call_target="tpu_custom_call" | custom-call | flops 18790481920 | bytes 14680064 | tf_op jit(solution)/shard_map/dispatch/pallas_call | solution.py:330
  124.2 0.0 copy-done
  124.2 118.1 %combine.1 = bf16[128,7168]{1,0:T(8,128)(2,1)} custom-call(bf16[2,2,320,512]{3,2,1,0:T(8,128)(2,1)} %dispatch.1.hid, bf16[512,7168]{1,0:T(8,128)(2,1)} %bitcast.18, s32[128,2]{1,0:T(8,128)} %copy-done, f32[128,2]{1,0:T(8,128)} %bitcast.15, bf16[128,7168]{1,0:T(8,128)(2,1)} %bitcast.20), custom_call_target="tpu_custom_call" | custom-call | flops 9395240960 | bytes 7340032 | tf_op jit(solution)/shard_map/combine/pallas_call | solution.py:356
  242.3 2.8 %copy.19 = bf16[1,2,64,7168]{3,2,1,0:T(8,128)(2,1)} copy(bf16[1,2,64,7168]{3,2,1,0:T(8,128)(2,1)} %bitcast.13) | data formatting | bytes 3670016
  (2 shorter events, 0.0 us)
Async XLA Ops:
  3.7 120.5 %copy-start = (s32[128,2]{1,0:T(8,128)}, s32[128,2]{1,0:T(8,128)S(1)}, u32[]{:S(2)}) copy-start(s32[128,2]{1,0:T(8,128)S(1)} %fusion.target) | copy-start | bytes 3076
